TPU v7x, 512 devices: a whole 4x4x16 slice. The times are simulated.
512 devices in a mesh: ctx: 64 (over y, z), tp: 8 (over x, core).
Axes of the slice: x: 4, y: 4, z: 16, core: 2. Of those that a mesh axis runs over, the one named last changes fastest.
Arguments:
- query_rows: bfloat16 [8192, 4096], P('ctx', 'tp'), may hold values from -6 to 6
- key_rows: bfloat16 [8192, 4096], P('ctx', 'tp'), may hold values from -0.5 to 0.5
- value_rows: bfloat16 [8192, 4096], P('ctx', 'tp'), may hold values from -40 to 40
- position: int32 [8192], P('ctx'), may hold values from 0 to 8191, as said below
- lengths: int32 [32], replicated, may hold values from 1 to 512, 8192 in all
- decay_rates: float32 [32], P('tp'), may hold values from 0.0001953125 to 0.0333333333
- norm_gain: float32 [4096], P('tp'), may hold values from 0.5 to 1.5
- grad_output: bfloat16 [8192, 4096], P('ctx', 'tp'), may hold values from -6 to 6
Outputs:
- normed: bfloat16 [8192, 4096], P('ctx', 'tp')
- grad_query: bfloat16 [8192, 4096], P('ctx', 'tp')
- grad_key: bfloat16 [8192, 4096], P('ctx', 'tp')
- grad_value: bfloat16 [8192, 4096], P('ctx', 'tp')
Inputs may be any that keep to these rules, and one draw needn't show every extreme that they name: position is a permutation of the 8192 places; among the rows of one device at most 4 lie in one block of 128 places, and in every draw every device has a block with exactly 4. lengths sum to 8192; the longest is exactly 512.
All inputs are finite; a program needn't handle non-finite values.
Results may differ from a plain program's by a relative error of at most 0.012.
Values may be sent and summed in bfloat16 or wider, within the bound.
A program may use at most 128 MiB of HBM per device.

v0:
```python
import jax
import jax.numpy as jnp
from jax import lax
from jax.sharding import PartitionSpec as P

epsilon = 1e-05
highest = lax.Precision.HIGHEST


def entering(value, axis, join, neutral, backward):
    count, mine = (lax.axis_size(axis), lax.axis_index(axis))
    pieces = jax.tree.map(lambda part: lax.all_gather(part, axis), value)
    if backward:
        pieces = jax.tree.map(lambda part: part[::-1], pieces)
        mine = count - 1 - mine
    running = jax.tree.map(
        lambda part, zero: jnp.full_like(part, 0) + jnp.asarray(zero, part.dtype), value, neutral
    )

    def turn(position, running):
        longer = join(running, jax.tree.map(lambda part: part[position], pieces))
        return jax.tree.map(lambda new, old: jnp.where(position < mine, new, old), longer, running)

    return lax.fori_loop(0, count - 1, turn, running)


def doc_index(doc_starts, places):
    return jnp.sum((doc_starts[None, :] <= places[:, None]).astype(jnp.int32), axis=1) - 1


def block_masks(doc_ids, doc_prev, doc_next, decay_rates, row_pos, block_rows):
    row_gap = row_pos[:, None] - row_pos[None, :]
    causal = row_gap >= 0.0
    decay_grid = jnp.exp(-decay_rates[:, None, None] * jnp.maximum(row_gap, 0.0)[None, :, :])
    same_doc = (doc_ids[:, None] == doc_ids[None, :]) & causal
    weight = jnp.where(same_doc[None, :, :], decay_grid, 0.0)
    enter_weight = jnp.where(
        (doc_ids == doc_prev)[:, None],
        jnp.exp(-decay_rates[None, :] * (row_pos[:, None] + 1.0)),
        0.0,
    )
    leave_weight = jnp.where(
        (doc_ids == doc_next)[:, None],
        jnp.exp(-decay_rates[None, :] * (block_rows - row_pos[:, None])),
        0.0,
    )
    own_end = jnp.where(
        (doc_ids == doc_ids[-1])[:, None],
        jnp.exp(-decay_rates[None, :] * (block_rows - 1.0 - row_pos[:, None])),
        0.0,
    )
    own_start = jnp.where(
        (doc_ids == doc_ids[0])[:, None], jnp.exp(-decay_rates[None, :] * row_pos[:, None]), 0.0
    )
    span_decay = jnp.exp(-decay_rates * block_rows)
    fwd_factor = jnp.where(doc_prev == doc_ids[-1], span_decay, 0.0)
    bwd_factor = jnp.where(doc_ids[0] == doc_next, span_decay, 0.0)
    return (weight, enter_weight, leave_weight, own_end, own_start, fwd_factor, bwd_factor)


def combine(earlier, later):
    return (earlier[0] * later[0], later[0][:, None, None] * earlier[1] + later[1])


def body(query_rows, key_rows, value_rows, position, lengths, decay_rates, norm_gain, grad_output):
    block_rows, feat_width = query_rows.shape
    local_heads = decay_rates.shape[0]
    head_dim = feat_width // local_heads
    ctx_ranks = lax.axis_size("ctx")
    slot_count = 2 * block_rows // ctx_ranks
    owner_rank = position // block_rows
    within = position % block_rows
    onehot = (owner_rank[:, None] == jnp.arange(ctx_ranks, dtype=jnp.int32)[None, :]).astype(
        jnp.int32
    )
    order_in = jnp.sum(jnp.cumsum(onehot, axis=0) * onehot, axis=1) - 1
    slot_index = owner_rank * slot_count + order_in
    stacked = jnp.concatenate([query_rows, key_rows, value_rows], axis=1)
    send_rows = (
        jnp.zeros((ctx_ranks * slot_count, 3 * feat_width), stacked.dtype)
        .at[slot_index]
        .set(stacked)
    )
    send_places = (
        jnp.full((ctx_ranks * slot_count,), block_rows, jnp.int32).at[slot_index].set(within)
    )
    got_rows, got_places = (
        lax.all_to_all(
            send_rows.reshape(ctx_ranks, slot_count, 3 * feat_width),
            "ctx",
            split_axis=0,
            concat_axis=0,
            tiled=True,
        ),
        lax.all_to_all(
            send_places.reshape(ctx_ranks, slot_count),
            "ctx",
            split_axis=0,
            concat_axis=0,
            tiled=True,
        ),
    )
    flat_places = got_places.reshape(ctx_ranks * slot_count)
    packed = (
        jnp.zeros((block_rows, 3 * feat_width), stacked.dtype)
        .at[flat_places]
        .set(got_rows.reshape(ctx_ranks * slot_count, 3 * feat_width), mode="drop")
    )
    shape_three = (block_rows, local_heads, head_dim)
    query_block = packed[:, :feat_width].reshape(shape_three)
    key_block = packed[:, feat_width : 2 * feat_width].reshape(shape_three)
    value_block = packed[:, 2 * feat_width :].reshape(shape_three)
    total_tokens = block_rows * ctx_ranks
    my_start = lax.axis_index("ctx") * block_rows
    doc_starts = jnp.cumsum(lengths) - lengths
    doc_ids = doc_index(doc_starts, my_start + jnp.arange(block_rows, dtype=jnp.int32))
    edges = jnp.stack([my_start - 1, jnp.minimum(my_start + block_rows, total_tokens - 1)])
    edge_ids = doc_index(doc_starts, edges)
    doc_prev = edge_ids[0]
    doc_next = jnp.where(my_start + block_rows < total_tokens, edge_ids[1], -2)
    row_pos = jnp.arange(block_rows, dtype=jnp.float32)
    weight, enter_weight, leave_weight, own_end, own_start, fwd_factor, bwd_factor = block_masks(
        doc_ids, doc_prev, doc_next, decay_rates, row_pos, block_rows
    )
    query_f = query_block.astype(jnp.float32)
    key_f = key_block.astype(jnp.float32)
    value_f = value_block.astype(jnp.float32)
    scores = jnp.einsum("phd,shd->hps", query_block, key_block, preferred_element_type=jnp.float32)
    probs_bf = (scores * weight).astype(jnp.bfloat16)
    intra_term = jnp.einsum(
        "hps,shd->phd", probs_bf, value_block, preferred_element_type=jnp.float32
    )
    local_state = jnp.einsum(
        "shd,she->hde",
        key_f * own_end[:, :, None],
        value_f,
        precision=highest,
        preferred_element_type=jnp.float32,
    )
    identity_pair = (jnp.ones_like(fwd_factor), jnp.zeros_like(local_state))
    prefix = entering((fwd_factor, local_state), "ctx", combine, identity_pair, False)
    state_in = prefix[1]
    inter_term = jnp.einsum(
        "phd,hde->phe",
        query_f * enter_weight[:, :, None],
        state_in,
        precision=highest,
        preferred_element_type=jnp.float32,
    )
    attention = (intra_term + inter_term).astype(jnp.bfloat16).reshape(block_rows, feat_width)
    attn_f = attention.astype(jnp.float32)
    full_width = feat_width * lax.axis_size("tp")
    total_sq = lax.psum(jnp.sum(attn_f * attn_f, axis=1), "tp")
    inverse = lax.rsqrt(total_sq / full_width + epsilon)
    normed = (attn_f * inverse[:, None] * norm_gain).astype(jnp.bfloat16)
    grad_f = grad_output.astype(jnp.float32) * norm_gain
    cross_sum = lax.psum(jnp.sum(grad_f * attn_f, axis=1), "tp")
    grad_attn = (
        (inverse[:, None] * grad_f - attn_f * (inverse**3 * cross_sum / full_width)[:, None])
        .astype(jnp.bfloat16)
        .reshape(shape_three)
    )
    grad_attn_f = grad_attn.astype(jnp.float32)
    grad_scores = jnp.einsum(
        "phd,shd->hps", grad_attn, value_block, preferred_element_type=jnp.float32
    )
    grad_probs = (grad_scores * weight).astype(jnp.bfloat16)
    local_back = jnp.einsum(
        "phd,phe->hde",
        query_f * own_start[:, :, None],
        grad_attn_f,
        precision=highest,
        preferred_element_type=jnp.float32,
    )
    identity_back = (jnp.ones_like(bwd_factor), jnp.zeros_like(local_back))
    suffix = entering((bwd_factor, local_back), "ctx", combine, identity_back, True)
    state_out = suffix[1]
    grad_q = jnp.einsum(
        "hps,shd->phd", grad_probs, key_block, preferred_element_type=jnp.float32
    ) + jnp.einsum(
        "phe,hde->phd",
        grad_attn_f * enter_weight[:, :, None],
        state_in,
        precision=highest,
        preferred_element_type=jnp.float32,
    )
    grad_k = jnp.einsum(
        "hps,phd->shd", grad_probs, query_block, preferred_element_type=jnp.float32
    ) + jnp.einsum(
        "she,hde->shd",
        value_f * leave_weight[:, :, None],
        state_out,
        precision=highest,
        preferred_element_type=jnp.float32,
    )
    grad_v = jnp.einsum(
        "hps,phd->shd", probs_bf, grad_attn, preferred_element_type=jnp.float32
    ) + jnp.einsum(
        "shd,hde->she",
        key_f * leave_weight[:, :, None],
        state_out,
        precision=highest,
        preferred_element_type=jnp.float32,
    )
    grad_packed = jnp.concatenate(
        [
            grad_q.astype(jnp.bfloat16).reshape(block_rows, feat_width),
            grad_k.astype(jnp.bfloat16).reshape(block_rows, feat_width),
            grad_v.astype(jnp.bfloat16).reshape(block_rows, feat_width),
        ],
        axis=1,
    )
    back_rows = grad_packed[jnp.minimum(flat_places, block_rows - 1)].reshape(
        ctx_ranks, slot_count, 3 * feat_width
    )
    returned = lax.all_to_all(back_rows, "ctx", split_axis=0, concat_axis=0, tiled=True)
    mine = returned.reshape(ctx_ranks * slot_count, 3 * feat_width)[slot_index]
    return (
        normed,
        mine[:, :feat_width],
        mine[:, feat_width : 2 * feat_width],
        mine[:, 2 * feat_width :],
    )


def solution(mesh):
    in_specs = (
        P("ctx", "tp"),
        P("ctx", "tp"),
        P("ctx", "tp"),
        P("ctx"),
        P(),
        P("tp"),
        P("tp"),
        P("ctx", "tp"),
    )
    out_specs = (P("ctx", "tp"), P("ctx", "tp"), P("ctx", "tp"), P("ctx", "tp"))
    return jax.shard_map(body, mesh=mesh, in_specs=in_specs, out_specs=out_specs, check_vma=False)
```

profile of v0, /device:TPU:1, one launch (start us, length us, event | category | flops | bytes accessed | tf_op | source)
XLA Modules:
  0.0 696.0 jit_solution(4382999979151844540)
XLA Ops:
  10.0 19.3 %all-to-all-start = ((s32[64,1,4]{2,1,0:T(1,128)}), s32[64,1,4]{2,1,0:T(1,128)S(1)}, u32[]{:S(2)}, u32[]{:S(2)}) async-start(s32[64,1,4]{2,1,0:T(1,128)} %bitcast), calls=%async_computation | async-start | bytes 65536 | tf_op jit(solution)/shard_map/all_to_all | solution.py:95
  29.3 2.0 scatter_custom_fusion.1
  31.3 1.1 reshape.380
  32.3 10.2 %all-to-all-done = s32[64,1,4]{2,1,0:T(1,128)S(1)} async-done(((s32[64,1,4]{2,1,0:T(1,128)}), s32[64,1,4]{2,1,0:T(1,128)S(1)}, u32[]{:S(2)}, u32[]{:S(2)}) %all-to-all-start) | async-done | bytes 1056 | tf_op jit(solution)/shard_map/all_to_all | solution.py:95
  42.5 4.6 all-to-all-start.1
  51.7 1.3 dynamic-slice
  54.4 1.9 broadcast_compare_fusion
  57.7 27.3 %all-to-all-done.1 = bf16[64,4,1536]{2,1,0:T(4,128)(2,1)S(1)} async-done(((bf16[64,4,1536]{2,1,0:T(4,128)(2,1)}), bf16[64,4,1536]{2,1,0:T(4,128)(2,1)S(1)}, u32[]{:S(2)}, u32[]{:S(2)}) %all-to-all-start.1) | async-done | bytes 786464 | tf_op jit(solution)/shard_map/all_to_all | solution.py:88
  85.2 1.9 scatter_custom_fusion.2
  87.3 1.1 fusion.16
  90.5 116.1 %all-reduce.2 = (f32[256]{0:T(256)S(1)}, f32[256]{0:T(256)S(1)}) all-reduce(f32[256]{0:T(256)S(1)} %fusion.41, f32[256]{0:T(256)S(1)} %get-tuple-element.290), channel_id=2, replica_groups=mesh['ctx'=64,'tp'=8] {'ctx'}, use_global_device_ids=true, to_apply=%add | all-reduce | flops 512 | bytes 4096
  208.4 71.5 %all-gather.7.cloned.1.call-done = f32[256,128,128]{2,1,0:T(8,128)} async-done(((f32[4,128,128]{2,1,0:T(8,128)}), f32[256,128,128]{2,1,0:T(8,128)}) %all-gather.7.cloned.1.call-update) | async-done | bytes 16777232 | tf_op jit(solution)/shard_map/all_gather | solution.py:12
  279.9 68.9 %while.28 = (s32[]{:T(128)}, f32[4,128,128]{2,1,0:T(8,128)S(1)}, s32[]{:T(128)}, f32[64,4]{1,0:T(8,128)S(1)}, f32[64,4,128,128]{3,2,1,0:T(8,128)}, /*index=5*/s32[]{:T(128)}, s32[]{:T(128)}) while((s32[]{:T(128)}, f32[4,128,128]{2,1,0:T(8,128)S(1)}, s32[]{:T(128)}, f32[64,4]{1,0:T(8,128)S(1)}, f32[64,4,128,128]{3,2,1,0:T(8,128)}, ...), condition=%wide.region_9.10_spmd.clone, body=%wide.region_8.9_spmd.clone.sunk | while | flops 262148 | bytes 786585 | solution.py:24
  281.0 1.1 fusion.74
  284.3 1.1 fusion.74
  350.3 12.9 %all-reduce.3 = (f32[128]{0:T(128)S(1)}, f32[128]{0:T(128)S(1)}) all-reduce(f32[128]{0:T(128)S(1)} %get-tuple-element.298, f32[128]{0:T(128)S(1)} %fusion.20), channel_id=1, replica_groups=mesh['ctx'=64,'tp'=8] {'tp'}, use_global_device_ids=true, to_apply=%region_11.12 | all-reduce | flops 256 | bytes 2048 | tf_op jit(solution)/shard_map/psum | solution.py:153
  364.0 1.1 fusion.17
  366.6 187.3 %all-gather.9.cloned.1.call-done = f32[256,128,128]{2,1,0:T(8,128)} async-done(((f32[4,128,128]{2,1,0:T(8,128)}), f32[256,128,128]{2,1,0:T(8,128)}) %all-gather.9.cloned.1.call-update) | async-done | bytes 16777232 | tf_op jit(solution)/shard_map/all_gather | solution.py:12
  553.9 11.6 %rev.7 = f32[64,4,128,128]{3,2,1,0:T(8,128)} reverse(f32[64,4,128,128]{3,2,1,0:T(8,128)} %bitcast.80), dimensions={0} | reverse | bytes 33554432 | tf_op jit(solution)/shard_map/rev | solution.py:14
  565.6 68.9 %while.29 = (s32[]{:T(128)}, f32[4,128,128]{2,1,0:T(8,128)S(1)}, s32[]{:T(128)}, f32[64,4]{1,0:T(8,128)S(1)}, f32[64,4,128,128]{3,2,1,0:T(8,128)}, /*index=5*/s32[]{:T(128)}, s32[]{:T(128)}) while((s32[]{:T(128)}, f32[4,128,128]{2,1,0:T(8,128)S(1)}, s32[]{:T(128)}, f32[64,4]{1,0:T(8,128)S(1)}, f32[64,4,128,128]{3,2,1,0:T(8,128)}, ...), condition=%wide.region_15.16_spmd.clone, body=%wide.region_14.15_spmd.clone.sunk | while | flops 262148 | bytes 786585 | solution.py:24
  635.8 1.3 gather_fusion
  637.0 1.1 reshape.391
  638.1 10.4 %all-to-all-start.2 = ((bf16[64,4,1536]{2,1,0:T(4,128)(2,1)}), bf16[64,4,1536]{2,1,0:T(4,128)(2,1)S(1)}, u32[]{:S(2)}, u32[]{:S(2)}) async-start(bf16[64,4,1536]{2,1,0:T(4,128)(2,1)} %reshape.391), calls=%async_computation.2 | async-start | bytes 1572864 | tf_op jit(solution)/shard_map/all_to_all | solution.py:216
  649.3 38.0 %all-to-all-done.2 = bf16[64,4,1536]{2,1,0:T(4,128)(2,1)S(1)} async-done(((bf16[64,4,1536]{2,1,0:T(4,128)(2,1)}), bf16[64,4,1536]{2,1,0:T(4,128)(2,1)S(1)}, u32[]{:S(2)}, u32[]{:S(2)}) %all-to-all-start.2) | async-done | bytes 786464 | tf_op jit(solution)/shard_map/all_to_all | solution.py:216
  (320 shorter events, 150.5 us)
Async XLA Ops:
  10.0 32.5 %all-to-all-start = ((s32[64,1,4]{2,1,0:T(1,128)}), s32[64,1,4]{2,1,0:T(1,128)S(1)}, u32[]{:S(2)}, u32[]{:S(2)}) async-start(s32[64,1,4]{2,1,0:T(1,128)} %bitcast), calls=%async_computation | async-start | bytes 65536 | tf_op jit(solution)/shard_map/all_to_all | solution.py:95
  42.5 42.5 %all-to-all-start.1 = ((bf16[64,4,1536]{2,1,0:T(4,128)(2,1)}), bf16[64,4,1536]{2,1,0:T(4,128)(2,1)S(1)}, u32[]{:S(2)}, u32[]{:S(2)}) async-start(bf16[64,4,1536]{2,1,0:T(4,128)(2,1)} %reshape.380), calls=%async_computation.1 | async-start | bytes 1572864 | tf_op jit(solution)/shard_map/all_to_all | solution.py:88
  47.1 232.8 %all-gather.7.cloned.1.call-start = ((), (), s32[]{:S(2)}) async-start(), calls=%async_computation.3 | async-start | bytes 17039360 | tf_op jit(solution)/shard_map/all_gather | solution.py:12
  88.4 465.5 %all-gather.9.cloned.1.call-start = ((), (), s32[]{:S(2)}) async-start(), calls=%async_computation.4 | async-start | bytes 17039360 | tf_op jit(solution)/shard_map/all_gather | solution.py:12
  638.1 49.2 %all-to-all-start.2 = ((bf16[64,4,1536]{2,1,0:T(4,128)(2,1)}), bf16[64,4,1536]{2,1,0:T(4,128)(2,1)S(1)}, u32[]{:S(2)}, u32[]{:S(2)}) async-start(bf16[64,4,1536]{2,1,0:T(4,128)(2,1)} %reshape.391), calls=%async_computation.2 | async-start | bytes 1572864 | tf_op jit(solution)/shard_map/all_to_all | solution.py:216
Sparse Core Ops, SparseCore 0:
  88.5 191.3 all-gather.6
  365.3 188.6 all-gather.8
where the time goes:
time: 704 us; the launch traced here: 696 us
  waiting for transfers between devices  334 us (47%)
  other arithmetic  143 us (20%)
  blocking collectives  129 us (18%)
  starting transfers between devices  34.4 us (5%)
  local copies, waits for them, and re-layouts  28.3 us (4%)
  between operations  17.6 us (3%)
    all_gather x2, waiting for transfers between devices, entering(): pieces = jax.tree.map(lambda part: lax.all_gather(part, axis), value)  259 us
    select_n x126, other arithmetic, turn(): jnp.where(position < mine, new, old)  133 us
    unnamed x1, blocking collectives  116 us
    all_to_all x1, waiting for transfers between devices, body(): lax.all_to_all(back_rows, 'ctx', split_axis=0, concat_axis=0, tiled=True)  38 us
    all_to_all x1, waiting for transfers between devices, body(): lax.all_to_all(send_rows.reshape(ctx_ranks, slot_count, 3 * feat_width),...  27.3 us
    all_to_all x1, starting transfers between devices, body(): lax.all_to_all(send_places.reshape(ctx_ranks, slot_count), 'ctx', split_a...  19.3 us
  transfers between devices with their start and end apart: 5, of which 5 were waited for; matrix products, arithmetic and copies ran while one was open for 2% of the time, Pallas kernels for 0%

commit v1 on v0

v1 whole, which is shorter than its diff:
```python
import jax
import jax.numpy as jnp
from jax import lax
from jax.experimental import pallas as pl
from jax.experimental.pallas import tpu as pltpu
from jax.sharding import PartitionSpec as P

MESH = pl.DeviceIdType.MESH
F32, BF16, I32 = jnp.float32, jnp.bfloat16, jnp.int32
HIGHEST = lax.Precision.HIGHEST
EPSILON = 1e-05
ROWS = 128
HD = 128
JOIN = 4
SPAN = JOIN * ROWS
CTX, TP = 64, 8
GROUPS = CTX // JOIN
CAP = 4 * JOIN
SLOTS = GROUPS * CAP
ARRIVE = CTX * CAP
WIDE = 3 * HD


def dot(a, b, precision=None):
    return jnp.dot(a, b, preferred_element_type=F32, precision=precision)


def dot_nt(a, b, precision=None):
    return lax.dot_general(a, b, (((1,), (1,)), ((), ())), preferred_element_type=F32, precision=precision)


def dot_tn(a, b):
    return lax.dot_general(a, b, (((0,), (0,)), ((), ())), preferred_element_type=F32)


def iota(shape, dim):
    return lax.broadcasted_iota(I32, shape, dim)


def onehot(condition):
    return jnp.where(condition, 1.0, 0.0).astype(BF16)


def column(row):
    return jnp.broadcast_to(row, (ROWS, ROWS)).T


def kernel(
    pos_ref, len_ref, rate_ref, gain_ref, q_ref, k_ref, v_ref, go_ref,
    nrm_ref, dq_ref, dk_ref, dv_ref,
    snd, rcv, snd2, rcv2, pls, plr, u_ref, ut_ref, w_ref, ends, qx, kx, vx, gox, att, dob, pb, dpb,
    nsend, state, state_in, back, back_in, part, ar1, sub, ar2, ssem, rsem,
):
    c, t = lax.axis_index("ctx"), lax.axis_index("tp")
    grp, k = c // JOIN, lax.rem(c, JOIN)
    own_cols = pl.ds(pl.multiple_of(k * HD, HD), HD)

    barrier = pltpu.get_barrier_semaphore()

    @pl.loop(1, CTX)
    def _(d):
        pl.semaphore_signal(barrier, inc=1, device_id={"ctx": lax.rem(c + d, CTX)}, device_id_type=MESH)

    @pl.loop(1, TP)
    def _(d):
        pl.semaphore_signal(barrier, inc=1, device_id={"tp": lax.rem(t + d, TP)}, device_id_type=MESH)

    def remote(src, dst, index, **where):
        return pltpu.make_async_remote_copy(
            src_ref=src, dst_ref=dst, send_sem=ssem.at[index], recv_sem=rsem.at[index],
            device_id=where, device_id_type=MESH,
        )

    def wait(ref, sems, index):
        pltpu.make_async_copy(ref, ref, sems.at[index]).wait()

    def peer(d):
        f = CTX - d
        turn, dy = f // 4, lax.rem(f, 4)
        h = (turn + 1) // 2
        dz = jnp.where(lax.rem(turn, 2) == 1, h, 16 - h)
        return lax.rem(c // 16 + dy, 4) * 16 + lax.rem(lax.rem(c, 16) + dz, 16)

    pos = pos_ref[...]
    posr = jnp.broadcast_to(pos, (ROWS, ROWS))
    posc = posr.T
    gr, gc = posr >> 9, posc >> 9
    ri, ci = iota((ROWS, ROWS), 0), iota((ROWS, ROWS), 1)
    same = gr == gc
    rank_row = jnp.sum(jnp.where(same & (ri < ci), 1, 0), axis=0, keepdims=True)
    rank_col = jnp.sum(jnp.where(same & (ci < ri), 1, 0), axis=1, keepdims=True)
    slot_row = gr[:1] * CAP + rank_row
    slot_col = gc[:, :1] * CAP + rank_col
    place = (pos & (SPAN - 1)) + 1
    holds = jnp.where(iota((GROUPS, ROWS), 0) == gr[:1], place, 0).astype(F32)
    ranked = jnp.where(ci == rank_col, 1.0, 0.0)
    pls[...] = dot(holds, ranked, HIGHEST) - 1.0
    pick = onehot(iota((SLOTS, ROWS), 0) == slot_row)

    def spread(ref, part_index):
        moved = dot(pick, ref[...]).astype(BF16)
        for h in range(JOIN):
            snd[:, h, :, part_index * HD : (part_index + 1) * HD] = moved[:, h * HD : (h + 1) * HD].reshape(
                GROUPS, CAP, HD
            )

    spread(k_ref, 0)
    spread(v_ref, 1)
    spread(q_ref, 2)
    pl.semaphore_wait(barrier, CTX - 1 + TP - 1)

    @pl.loop(1, CTX)
    def _(d):
        p = peer(d)
        remote(pls.at[pl.ds(p // JOIN, 1)], plr.at[pl.ds(c, 1)], 0, ctx=p).start()
        remote(
            snd.at[p // JOIN, lax.rem(p, JOIN), :, pl.ds(0, 2 * HD)],
            rcv.at[pl.ds(c * CAP, CAP), pl.ds(0, 2 * HD)],
            1, ctx=p,
        ).start()

    def mates(fn):
        for d in range(1, JOIN):
            m = lax.rem(k + d, JOIN)
            fn(m, grp * JOIN + m)

    mates(
        lambda m, p: remote(
            go_ref.at[:, pl.ds(pl.multiple_of(m * HD, HD), HD)], gox.at[pl.ds(k * ROWS, ROWS)], 3, ctx=p
        ).start()
    )

    @pl.loop(1, CTX)
    def _(d):
        p = peer(d)
        remote(
            snd.at[p // JOIN, lax.rem(p, JOIN), :, pl.ds(2 * HD, HD)],
            rcv.at[pl.ds(c * CAP, CAP), pl.ds(2 * HD, HD)],
            2, ctx=p,
        ).start()

    rcv[pl.ds(c * CAP, CAP)] = snd[grp, k]
    plr[pl.ds(c, 1)] = pls[pl.ds(grp, 1)]
    gox[pl.ds(k * ROWS, ROWS)] = go_ref[:, own_cols]

    rate = rate_ref[k]
    start = grp * SPAN
    here = iota((1, SPAN), 1) + start
    doc_row = jnp.full((1, SPAN), -1, I32)
    offset = jnp.int32(0)
    doc_prev, doc_next = jnp.int32(-1), jnp.int32(-1)
    doc_first, doc_last = jnp.int32(-1), jnp.int32(-1)
    for d in range(len_ref.shape[0]):
        doc_row += jnp.where(offset <= here, 1, 0)
        doc_prev += jnp.where(offset <= start - 1, 1, 0)
        doc_first += jnp.where(offset <= start, 1, 0)
        doc_last += jnp.where(offset <= start + SPAN - 1, 1, 0)
        doc_next += jnp.where(offset <= start + SPAN, 1, 0)
        offset += len_ref[d]
    doc_next = jnp.where(grp == GROUPS - 1, -2, doc_next)
    for i in range(JOIN):
        rows = slice(i * ROWS, (i + 1) * ROWS)
        doc_col = column(doc_row[:, rows])
        for j in range(i + 1):
            gap = (ri - ci) + (i - j) * ROWS
            kept = doc_col == doc_row[:, j * ROWS : (j + 1) * ROWS]
            if i == j:
                kept = kept & (gap >= 0)
            decay = jnp.exp(-rate * jnp.maximum(gap, 0).astype(F32))
            w_ref[rows, j * ROWS : (j + 1) * ROWS] = jnp.where(kept, decay, 0.0)
        at = (ri + i * ROWS).astype(F32)
        ends[0, rows] = jnp.where(doc_col == doc_prev, jnp.exp(-rate * (at + 1.0)), 0.0)
        ends[1, rows] = jnp.where(doc_col == doc_next, jnp.exp(-rate * (SPAN - at)), 0.0)
        ends[2, rows] = jnp.where(doc_col == doc_last, jnp.exp(-rate * (SPAN - 1.0 - at)), 0.0)
        ends[3, rows] = jnp.where(doc_col == doc_first, jnp.exp(-rate * at), 0.0)

    wait(plr.at[pl.ds(0, CTX - 1)], rsem, 0)
    places = plr[...]
    tile = jnp.where(lax.rem(iota((ROWS, ARRIVE), 1), CAP) == iota((ROWS, ARRIVE), 0), 1.0, 0.0)
    owner = iota((CTX, ARRIVE), 1) // CAP == iota((CTX, ARRIVE), 0)
    place_row = jnp.sum(jnp.where(owner, dot(places, tile, HIGHEST), 0.0), axis=0, keepdims=True)
    place_row = place_row.astype(I32)
    for i in range(JOIN):
        rows = slice(i * ROWS, (i + 1) * ROWS)
        u_ref[rows] = onehot(iota((ROWS, ARRIVE), 0) + i * ROWS == place_row)
    for j in range(ARRIVE // ROWS):
        cols = slice(j * ROWS, (j + 1) * ROWS)
        place_col = column(place_row[:, cols])
        for i in range(JOIN):
            ut_ref[cols, i * ROWS : (i + 1) * ROWS] = onehot(place_col == ci + i * ROWS)

    wait(rcv.at[pl.ds(0, ARRIVE - CAP), pl.ds(0, 2 * HD)], rsem, 1)
    kv = dot(u_ref[...], rcv[:, : 2 * HD]).astype(BF16)
    kx[...] = kv[:, :HD]
    vx[...] = kv[:, HD:]
    state[...] = dot_tn((kx[...].astype(F32) * ends[2]).astype(BF16), vx[...]).astype(BF16)
    remote(state, state_in, 4, ctx=lax.rem(c + JOIN, CTX)).start()

    wait(rcv.at[pl.ds(0, ARRIVE - CAP), pl.ds(2 * HD, HD)], rsem, 2)
    qx[...] = dot(u_ref[...], rcv[:, 2 * HD :]).astype(BF16)
    for i in range(JOIN):
        rows, n = slice(i * ROWS, (i + 1) * ROWS), (i + 1) * ROWS
        pb[rows, :n] = (dot_nt(qx[rows], kx[:n]) * w_ref[rows, :n]).astype(BF16)
    wait(gox.at[pl.ds(0, SPAN - ROWS)], rsem, 3)
    wait(state_in, rsem, 4)
    gain = gain_ref[:, own_cols]
    ones = jnp.ones((8, HD), F32)
    for i in range(JOIN):
        rows, n = slice(i * ROWS, (i + 1) * ROWS), (i + 1) * ROWS
        entered = (qx[rows].astype(F32) * ends[0, rows]).astype(BF16)
        a = (dot(pb[rows, :n], vx[:n]) + dot(entered, state_in[...])).astype(BF16)
        att[rows] = a
        a = a.astype(F32)
        g = gox[rows].astype(F32) * gain
        part[:, i * ROWS : (i + 1) * ROWS] = dot_nt(ones, a * a, HIGHEST)[:1]
        part[:, SPAN + i * ROWS : SPAN + (i + 1) * ROWS] = dot_nt(ones, g * a, HIGHEST)[:1]

    mates(lambda m, p: remote(part, ar1.at[k], 5, ctx=p).start())
    ar1[k] = part[...]
    wait(ar1.at[pl.ds(0, JOIN - 1)], rsem, 5)
    sub[...] = ar1[0] + ar1[1] + ar1[2] + ar1[3]
    for d in range(1, TP):
        remote(sub, ar2.at[t], 6, tp=lax.rem(t + d, TP)).start()
    ar2[t] = sub[...]
    wait(ar2.at[pl.ds(0, TP - 1)], rsem, 6)
    total = ar2[0]
    for d in range(1, TP):
        total += ar2[d]
    width = float(HD * JOIN * TP)
    inverse = lax.rsqrt(total[:, :SPAN] / width + EPSILON)
    coef = inverse * inverse * inverse * total[:, SPAN:] / width

    carried = jnp.zeros((HD, HD), F32)
    for i in range(JOIN):
        rows = slice(i * ROWS, (i + 1) * ROWS)
        inv, cf = column(inverse[:, rows]), column(coef[:, rows])
        a = att[rows].astype(F32)
        g = gox[rows].astype(F32) * gain
        d_o = (inv * g - a * cf).astype(BF16)
        dob[rows] = d_o
        nsend[i] = (a * inv * gain).astype(BF16)
        carried += dot_tn((qx[rows].astype(F32) * ends[3, rows]).astype(BF16), d_o)
    back[...] = carried.astype(BF16)
    remote(back, back_in, 8, ctx=lax.rem(c + CTX - JOIN, CTX)).start()

    def send_back(lo, n, index):
        @pl.loop(1, CTX)
        def _(d):
            p = peer(d)
            remote(
                snd2.at[pl.ds(p * CAP, CAP), pl.ds(lo, n)],
                rcv2.at[k, pl.ds(grp * CAP, CAP), pl.ds(lo, n)],
                index, ctx=p,
            ).start()

    dq = []
    for i in range(JOIN):
        rows, n = slice(i * ROWS, (i + 1) * ROWS), (i + 1) * ROWS
        dp = (dot_nt(dob[rows], vx[:n]) * w_ref[rows, :n]).astype(BF16)
        dpb[rows, :n] = dp
        entered = (dob[rows].astype(F32) * ends[0, rows]).astype(BF16)
        dq.append((dot(dp, kx[:n]) + dot_nt(entered, state_in[...])).astype(BF16))
    snd2[:, :HD] = dot(ut_ref[...], jnp.concatenate(dq, axis=0)).astype(BF16)
    send_back(0, HD, 9)
    mates(lambda m, p: remote(nsend.at[m], nrm_ref.at[:, own_cols], 7, ctx=p).start())
    nrm_ref[:, own_cols] = nsend[k]

    wait(back_in, rsem, 8)
    dk, dv = [], []
    for j in range(JOIN):
        cols, low = slice(j * ROWS, (j + 1) * ROWS), j * ROWS
        leave = ends[1, cols]
        value = (vx[cols].astype(F32) * leave).astype(BF16)
        key = (kx[cols].astype(F32) * leave).astype(BF16)
        dk.append((dot_tn(dpb[low:, cols], qx[low:]) + dot_nt(value, back_in[...])).astype(BF16))
        dv.append((dot_tn(pb[low:, cols], dob[low:]) + dot(key, back_in[...])).astype(BF16))
    both = jnp.concatenate([jnp.concatenate(dk, axis=0), jnp.concatenate(dv, axis=0)], axis=1)
    snd2[:, HD:] = dot(ut_ref[...], both).astype(BF16)
    send_back(HD, 2 * HD, 10)
    rcv2[k, pl.ds(grp * CAP, CAP)] = snd2[pl.ds(c * CAP, CAP)]

    give = onehot(iota((ROWS, SLOTS), 1) == slot_col)
    wait(snd2.at[pl.ds(0, ARRIVE - CAP), pl.ds(0, HD)], rsem, 9)
    for h in range(JOIN):
        dq_ref[:, h * HD : (h + 1) * HD] = dot(give, rcv2[h, :, :HD]).astype(BF16)
    wait(snd2.at[pl.ds(0, ARRIVE - CAP), pl.ds(HD, 2 * HD)], rsem, 10)
    for h in range(JOIN):
        moved = dot(give, rcv2[h, :, HD:]).astype(BF16)
        dk_ref[:, h * HD : (h + 1) * HD] = moved[:, :HD]
        dv_ref[:, h * HD : (h + 1) * HD] = moved[:, HD:]
    wait(nsend.at[pl.ds(0, JOIN - 1)], rsem, 7)

    wait(plr.at[pl.ds(0, CTX - 1)], ssem, 0)
    wait(rcv.at[pl.ds(0, ARRIVE - CAP), pl.ds(0, 2 * HD)], ssem, 1)
    wait(rcv.at[pl.ds(0, ARRIVE - CAP), pl.ds(2 * HD, HD)], ssem, 2)
    wait(gox.at[pl.ds(0, SPAN - ROWS)], ssem, 3)
    wait(state, ssem, 4)
    wait(ar1.at[pl.ds(0, JOIN - 1)], ssem, 5)
    wait(ar2.at[pl.ds(0, TP - 1)], ssem, 6)
    wait(nsend.at[pl.ds(0, JOIN - 1)], ssem, 7)
    wait(back, ssem, 8)
    wait(snd2.at[pl.ds(0, ARRIVE - CAP), pl.ds(0, HD)], ssem, 9)
    wait(snd2.at[pl.ds(0, ARRIVE - CAP), pl.ds(HD, 2 * HD)], ssem, 10)


def body(query_rows, key_rows, value_rows, position, lengths, decay_rates, norm_gain, grad_output):
    vmem, smem = pl.BlockSpec(memory_space=pltpu.VMEM), pl.BlockSpec(memory_space=pltpu.SMEM)
    shape = jax.ShapeDtypeStruct(query_rows.shape, BF16)
    return pl.pallas_call(
        kernel,
        out_shape=(shape,) * 4,
        in_specs=[vmem, smem, smem] + [vmem] * 5,
        out_specs=(vmem,) * 4,
        scratch_shapes=[
            pltpu.VMEM((GROUPS, JOIN, CAP, WIDE), BF16),
            pltpu.VMEM((ARRIVE, WIDE), BF16),
            pltpu.VMEM((ARRIVE, WIDE), BF16),
            pltpu.VMEM((JOIN, SLOTS, WIDE), BF16),
            pltpu.VMEM((GROUPS, ROWS), F32),
            pltpu.VMEM((CTX, ROWS), F32),
            pltpu.VMEM((SPAN, ARRIVE), BF16),
            pltpu.VMEM((ARRIVE, SPAN), BF16),
            pltpu.VMEM((SPAN, SPAN), F32),
            pltpu.VMEM((4, SPAN, HD), F32),
            pltpu.VMEM((SPAN, HD), BF16),
            pltpu.VMEM((SPAN, HD), BF16),
            pltpu.VMEM((SPAN, HD), BF16),
            pltpu.VMEM((SPAN, HD), BF16),
            pltpu.VMEM((SPAN, HD), BF16),
            pltpu.VMEM((SPAN, HD), BF16),
            pltpu.VMEM((SPAN, SPAN), BF16),
            pltpu.VMEM((SPAN, SPAN), BF16),
            pltpu.VMEM((JOIN, ROWS, HD), BF16),
            pltpu.VMEM((HD, HD), BF16),
            pltpu.VMEM((HD, HD), BF16),
            pltpu.VMEM((HD, HD), BF16),
            pltpu.VMEM((HD, HD), BF16),
            pltpu.VMEM((1, 2 * SPAN), F32),
            pltpu.VMEM((JOIN, 1, 2 * SPAN), F32),
            pltpu.VMEM((1, 2 * SPAN), F32),
            pltpu.VMEM((TP, 1, 2 * SPAN), F32),
            pltpu.SemaphoreType.DMA((11,)),
            pltpu.SemaphoreType.DMA((11,)),
        ],
        compiler_params=pltpu.CompilerParams(
            collective_id=0, has_side_effects=True, vmem_limit_bytes=40 << 20
        ),
        name="lightning",
    )(
        position.reshape(1, ROWS), lengths, decay_rates, norm_gain.reshape(1, -1),
        query_rows, key_rows, value_rows, grad_output,
    )


def solution(mesh):
    rows, specs = P("ctx", "tp"), (P("ctx", "tp"),) * 4
    return jax.shard_map(
        body,
        mesh=mesh,
        in_specs=(rows, rows, rows, P("ctx"), P(), P("tp"), P("tp"), rows),
        out_specs=specs,
        check_vma=False,
    )
```

time: 704 us -> 122 us (0.17); the launches traced: 696 us -> 122 us
  waiting for transfers between devices: 334 us -> 0 us
  other arithmetic: 143 us -> 0 us
  blocking collectives: 129 us -> 0 us
  Pallas kernels: 0 us -> 115 us
  starting transfers between devices: 34.4 us -> 0 us
  local copies, waits for them, and re-layouts: 28.3 us -> 6.91 us
  between operations: 17.6 us -> 0.68 us
    all_gather x2 -> x0, waiting for transfers between devices: 259 us -> none  [entering(): pieces = jax.tree.map(lambda part: lax.all_gather(part, axis), value)]
    select_n x130 -> x0, other arithmetic: 133 us -> none  [the longest x126 133 us: turn(): jnp.where(position < mine, new, old)]
    unnamed x1 -> x0, blocking collectives: 116 us -> none
    pallas_call x0 -> x1, Pallas kernels: none -> 115 us  [body(): pl.pallas_call(kernel, out_shape=(shape,) * 4, in_specs=[vmem, smem, smem...]
    all_to_all x3 -> x0, waiting for transfers between devices: 75.4 us -> none  [the longest x1 38 us: body(): lax.all_to_all(back_rows, 'ctx', split_axis=0, concat_axis=0, tiled=True)]
    all_to_all x3 -> x0, starting transfers between devices: 34.3 us -> none  [the longest x1 19.3 us: body(): lax.all_to_all(send_places.reshape(ctx_ranks, slot_count), 'ctx', split_a...]
    psum x1 -> x0, blocking collectives: 12.9 us -> none  [body(): total_sq = lax.psum(jnp.sum(attn_f * attn_f, axis=1), 'tp')]
    rev x2 -> x0, local copies, waits for them, and re-layouts: 11.6 us -> none  [entering(): pieces = jax.tree.map(lambda part: part[::-1], pieces)]
  transfers between devices with their start and end apart: 5 -> 0, of which waited for: 5 -> 0; matrix products, arithmetic and copies ran while one was open for 2% -> 0% of each run, Pallas kernels for 0% -> 0%
where the time goes in v1:
time: 122 us
  Pallas kernels  115 us (94%)
  local copies, waits for them, and re-layouts  6.91 us (6%)
    pallas_call x1, Pallas kernels, body(): pl.pallas_call(kernel, out_shape=(shape,) * 4, in_specs=[vmem, smem, smem...  115 us
    unnamed x20, local copies, waits for them, and re-layouts  6.91 us

profile of v1, /device:TPU:1, one launch (start us, length us, event | category | flops | bytes accessed | tf_op | source)
XLA Modules:
  0.0 122.1 jit_solution(11504272062213729455)
XLA Ops:
  0.6 0.0 copy-start.4
  0.6 0.0 copy-start.5
  0.7 0.0 copy-start.6
  0.7 0.0 copy-start.7
  0.7 0.6 copy-done.4
  1.3 0.0 copy-done.5
  1.3 0.0 copy-done.6
  1.3 0.0 copy-done.7
  1.3 0.0 copy-start
  1.3 0.9 copy-done
  2.2 0.0 copy-start.1
  2.2 0.9 copy-done.1
  3.1 0.0 copy-start.2
  3.1 0.9 copy-done.2
  4.1 0.0 copy-start.3
  4.1 0.9 copy-done.3
  5.0 114.5 %lightning.1 = (bf16[128,512]{1,0:T(8,128)(2,1)S(1)}, bf16[128,512]{1,0:T(8,128)(2,1)S(1)}, bf16[128,512]{1,0:T(8,128)(2,1)S(1)}, bf16[128,512]{1,0:T(8,128)(2,1)S(1)}) custom-call(s32[1,128]{1,0:T(1,128)S(1)} %bitcast.3, s32[32]{0:T(128)S(1)} %copy-done.6, f32[4]{0:T(128)S(1)} %copy-done.7, f32[1,512]{1,0:T(1,128)S(1)} %bitcast.2, ...), custom_call_target="tpu_custom_call" | custom-call | tf_op jit(solution)/shard_map/lightning/pallas_call | solution.py:309
  119.5 0.7 copy.16
  120.2 0.7 copy.17
  120.8 0.7 copy.18
  121.5 0.7 copy.19
Async XLA Ops:
  0.6 0.7 copy-start.4
  0.6 0.7 copy-start.5
  0.7 0.7 copy-start.6
  0.7 0.7 copy-start.7
  1.3 0.9 copy-start
  2.2 0.9 copy-start.1
  3.1 0.9 copy-start.2
  4.1 0.9 copy-start.3

commit v2 on v1

--- a/solution.py
+++ b/solution.py
@@ -46,15 +46,27 @@
 
 
 def kernel(
-    pos_ref, len_ref, rate_ref, gain_ref, q_ref, k_ref, v_ref, go_ref,
-    nrm_ref, dq_ref, dk_ref, dv_ref,
-    snd, rcv, snd2, rcv2, pls, plr, u_ref, ut_ref, w_ref, ends, qx, kx, vx, gox, att, dob, pb, dpb,
-    nsend, state, state_in, back, back_in, part, ar1, sub, ar2, ssem, rsem,
+    pos_hbm, len_hbm, rate_hbm, gain_hbm, q_hbm, k_hbm, v_hbm, go_hbm,
+    nrm_out, dq_out, got, give_out,
+    pos_ref, len_ref, rate_ref, gain_ref, q_ref, k_ref, v_ref, go_ref, lsem,
+    snd, rcv, sndq, snd2, pall, u_ref, ut_ref, w_ref, ends, qx, kx, vx, gox, att, attx, dob, pb, dpb,
+    nrm_ref, dq_ref, give_ref, rcvq, state, state_in, back, back_in, part, ar1, sub, ar2, inv_ref, ssem, rsem,
 ):
     c, t = lax.axis_index("ctx"), lax.axis_index("tp")
     grp, k = c // JOIN, lax.rem(c, JOIN)
     own_cols = pl.ds(pl.multiple_of(k * HD, HD), HD)
 
+    loads = [
+        pltpu.make_async_copy(src, dst, lsem.at[i])
+        for i, (src, dst) in enumerate(
+            (
+                (pos_hbm, pos_ref), (k_hbm, k_ref), (v_hbm, v_ref), (q_hbm, q_ref),
+                (len_hbm, len_ref), (rate_hbm, rate_ref), (gain_hbm, gain_ref), (go_hbm, go_ref),
+            )
+        )
+    ]
+    for load in loads:
+        load.start()
     barrier = pltpu.get_barrier_semaphore()
 
     @pl.loop(1, CTX)
@@ -81,6 +93,7 @@
         dz = jnp.where(lax.rem(turn, 2) == 1, h, 16 - h)
         return lax.rem(c // 16 + dy, 4) * 16 + lax.rem(lax.rem(c, 16) + dz, 16)
 
+    loads[0].wait()
     pos = pos_ref[...]
     posr = jnp.broadcast_to(pos, (ROWS, ROWS))
     posc = posr.T
@@ -91,10 +104,6 @@
     rank_col = jnp.sum(jnp.where(same & (ci < ri), 1, 0), axis=1, keepdims=True)
     slot_row = gr[:1] * CAP + rank_row
     slot_col = gc[:, :1] * CAP + rank_col
-    place = (pos & (SPAN - 1)) + 1
-    holds = jnp.where(iota((GROUPS, ROWS), 0) == gr[:1], place, 0).astype(F32)
-    ranked = jnp.where(ci == rank_col, 1.0, 0.0)
-    pls[...] = dot(holds, ranked, HIGHEST) - 1.0
     pick = onehot(iota((SLOTS, ROWS), 0) == slot_row)
 
     def spread(ref, part_index):
@@ -104,43 +113,42 @@
                 GROUPS, CAP, HD
             )
 
-    spread(k_ref, 0)
-    spread(v_ref, 1)
-    spread(q_ref, 2)
+    for i, ref in enumerate((k_ref, v_ref, q_ref)):
+        loads[i + 1].wait()
+        spread(ref, i)
     pl.semaphore_wait(barrier, CTX - 1 + TP - 1)
 
-    @pl.loop(1, CTX)
+    own_y, own_z = c // 16, lax.rem(c, 16)
+
+    @pl.loop(1, 16)
     def _(d):
-        p = peer(d)
-        remote(pls.at[pl.ds(p // JOIN, 1)], plr.at[pl.ds(c, 1)], 0, ctx=p).start()
-        remote(
-            snd.at[p // JOIN, lax.rem(p, JOIN), :, pl.ds(0, 2 * HD)],
-            rcv.at[pl.ds(c * CAP, CAP), pl.ds(0, 2 * HD)],
-            1, ctx=p,
-        ).start()
+        remote(pos_ref, pall.at[pl.ds(c, 1)], 0, ctx=own_y * 16 + lax.rem(own_z + d, 16)).start()
+
+    def send_rows(lo, n, index):
+        @pl.loop(1, CTX)
+        def _(d):
+            p = peer(d)
+            remote(
+                snd.at[p // JOIN, lax.rem(p, JOIN), :, pl.ds(lo, n)],
+                rcv.at[pl.ds(c * CAP, CAP), pl.ds(lo, n)],
+                index, ctx=p,
+            ).start()
+
+    send_rows(0, 2 * HD, 1)
+    send_rows(2 * HD, HD, 2)
 
     def mates(fn):
         for d in range(1, JOIN):
             m = lax.rem(k + d, JOIN)
             fn(m, grp * JOIN + m)
 
-    mates(
-        lambda m, p: remote(
-            go_ref.at[:, pl.ds(pl.multiple_of(m * HD, HD), HD)], gox.at[pl.ds(k * ROWS, ROWS)], 3, ctx=p
-        ).start()
-    )
-
-    @pl.loop(1, CTX)
-    def _(d):
-        p = peer(d)
-        remote(
-            snd.at[p // JOIN, lax.rem(p, JOIN), :, pl.ds(2 * HD, HD)],
-            rcv.at[pl.ds(c * CAP, CAP), pl.ds(2 * HD, HD)],
-            2, ctx=p,
-        ).start()
-
     rcv[pl.ds(c * CAP, CAP)] = snd[grp, k]
-    plr[pl.ds(c, 1)] = pls[pl.ds(grp, 1)]
+    pall[pl.ds(c, 1)] = pos
+    give_ref[...] = onehot(iota((ROWS, SLOTS), 1) == slot_col)
+    stores = [pltpu.make_async_copy(give_ref, give_out, lsem.at[8])]
+    stores[0].start()
+    for load in loads[4:]:
+        load.wait()
     gox[pl.ds(k * ROWS, ROWS)] = go_ref[:, own_cols]
 
     rate = rate_ref[k]
@@ -174,11 +182,22 @@
         ends[2, rows] = jnp.where(doc_col == doc_last, jnp.exp(-rate * (SPAN - 1.0 - at)), 0.0)
         ends[3, rows] = jnp.where(doc_col == doc_first, jnp.exp(-rate * at), 0.0)
 
-    wait(plr.at[pl.ds(0, CTX - 1)], rsem, 0)
-    places = plr[...]
+    wait(pall.at[pl.ds(0, 15)], rsem, 0)
+    own_line = pall.at[pl.ds(pl.multiple_of(own_y * 16, 16), 16)]
+    for d in range(1, 4):
+        remote(own_line, own_line, 9, ctx=lax.rem(own_y + d, 4) * 16 + own_z).start()
+    wait(pall.at[pl.ds(0, 48)], rsem, 9)
+    everywhere = pall[...]
+    ours = everywhere >> 9 == grp
+    rank = dot(onehot(ours), onehot(ri < ci))
+    place = (everywhere & (SPAN - 1)).astype(F32) + 1.0
+    places = jnp.zeros((CTX, ROWS), F32)
+    for r in range(CAP):
+        held = jnp.sum(jnp.where(ours & (rank == float(r)), place, 0.0), axis=1, keepdims=True)
+        places = jnp.where(iota((CTX, ROWS), 1) == r, held, places)
     tile = jnp.where(lax.rem(iota((ROWS, ARRIVE), 1), CAP) == iota((ROWS, ARRIVE), 0), 1.0, 0.0)
     owner = iota((CTX, ARRIVE), 1) // CAP == iota((CTX, ARRIVE), 0)
-    place_row = jnp.sum(jnp.where(owner, dot(places, tile, HIGHEST), 0.0), axis=0, keepdims=True)
+    place_row = jnp.sum(jnp.where(owner, dot(places, tile, HIGHEST), 0.0), axis=0, keepdims=True) - 1.0
     place_row = place_row.astype(I32)
     for i in range(JOIN):
         rows = slice(i * ROWS, (i + 1) * ROWS)
@@ -197,38 +216,59 @@
     remote(state, state_in, 4, ctx=lax.rem(c + JOIN, CTX)).start()
 
     wait(rcv.at[pl.ds(0, ARRIVE - CAP), pl.ds(2 * HD, HD)], rsem, 2)
+    mates(
+        lambda m, p: remote(
+            go_ref.at[:, pl.ds(pl.multiple_of(m * HD, HD), HD)], gox.at[pl.ds(k * ROWS, ROWS)], 3, ctx=p
+        ).start()
+    )
     qx[...] = dot(u_ref[...], rcv[:, 2 * HD :]).astype(BF16)
     for i in range(JOIN):
         rows, n = slice(i * ROWS, (i + 1) * ROWS), (i + 1) * ROWS
         pb[rows, :n] = (dot_nt(qx[rows], kx[:n]) * w_ref[rows, :n]).astype(BF16)
-    wait(gox.at[pl.ds(0, SPAN - ROWS)], rsem, 3)
     wait(state_in, rsem, 4)
     gain = gain_ref[:, own_cols]
-    ones = jnp.ones((8, HD), F32)
+    ones = jnp.ones((8, HD), BF16)
+
+    def row_sums(x):
+        high = x.astype(BF16)
+        low = (x - high.astype(F32)).astype(BF16)
+        return (dot_nt(ones, high) + dot_nt(ones, low))[:1]
+
     for i in range(JOIN):
         rows, n = slice(i * ROWS, (i + 1) * ROWS), (i + 1) * ROWS
         entered = (qx[rows].astype(F32) * ends[0, rows]).astype(BF16)
         a = (dot(pb[rows, :n], vx[:n]) + dot(entered, state_in[...])).astype(BF16)
         att[rows] = a
         a = a.astype(F32)
+        part[:, i * ROWS : (i + 1) * ROWS] = row_sums(a * a)
+    wait(gox.at[pl.ds(0, SPAN - ROWS)], rsem, 3)
+    for i in range(JOIN):
+        rows = slice(i * ROWS, (i + 1) * ROWS)
         g = gox[rows].astype(F32) * gain
-        part[:, i * ROWS : (i + 1) * ROWS] = dot_nt(ones, a * a, HIGHEST)[:1]
-        part[:, SPAN + i * ROWS : SPAN + (i + 1) * ROWS] = dot_nt(ones, g * a, HIGHEST)[:1]
-
-    mates(lambda m, p: remote(part, ar1.at[k], 5, ctx=p).start())
-    ar1[k] = part[...]
-    wait(ar1.at[pl.ds(0, JOIN - 1)], rsem, 5)
-    sub[...] = ar1[0] + ar1[1] + ar1[2] + ar1[3]
+        part[:, SPAN + i * ROWS : SPAN + (i + 1) * ROWS] = row_sums(g * att[rows].astype(F32))
+
     for d in range(1, TP):
-        remote(sub, ar2.at[t], 6, tp=lax.rem(t + d, TP)).start()
-    ar2[t] = sub[...]
+        remote(part, ar2.at[t], 6, tp=lax.rem(t + d, TP)).start()
+    mates(
+        lambda m, p: remote(
+            att.at[pl.ds(pl.multiple_of(m * ROWS, ROWS), ROWS)], attx.at[:, own_cols], 7, ctx=p
+        ).start()
+    )
+    attx[:, own_cols] = att[pl.ds(pl.multiple_of(k * ROWS, ROWS), ROWS)]
+    ar2[t] = part[...]
     wait(ar2.at[pl.ds(0, TP - 1)], rsem, 6)
     total = ar2[0]
     for d in range(1, TP):
         total += ar2[d]
+    sub[...] = total
+    mates(lambda m, p: remote(sub, ar1.at[k], 5, ctx=p).start())
+    ar1[k] = total
+    wait(ar1.at[pl.ds(0, JOIN - 1)], rsem, 5)
+    total = ar1[0] + ar1[1] + ar1[2] + ar1[3]
     width = float(HD * JOIN * TP)
     inverse = lax.rsqrt(total[:, :SPAN] / width + EPSILON)
     coef = inverse * inverse * inverse * total[:, SPAN:] / width
+    inv_ref[...] = inverse
 
     carried = jnp.zeros((HD, HD), F32)
     for i in range(JOIN):
@@ -238,20 +278,15 @@
         g = gox[rows].astype(F32) * gain
         d_o = (inv * g - a * cf).astype(BF16)
         dob[rows] = d_o
-        nsend[i] = (a * inv * gain).astype(BF16)
         carried += dot_tn((qx[rows].astype(F32) * ends[3, rows]).astype(BF16), d_o)
     back[...] = carried.astype(BF16)
     remote(back, back_in, 8, ctx=lax.rem(c + CTX - JOIN, CTX)).start()
 
-    def send_back(lo, n, index):
+    def send_back(src, dst, index):
         @pl.loop(1, CTX)
         def _(d):
             p = peer(d)
-            remote(
-                snd2.at[pl.ds(p * CAP, CAP), pl.ds(lo, n)],
-                rcv2.at[k, pl.ds(grp * CAP, CAP), pl.ds(lo, n)],
-                index, ctx=p,
-            ).start()
+            remote(src.at[pl.ds(p * CAP, CAP)], dst.at[k, pl.ds(grp * CAP, CAP)], index, ctx=p).start()
 
     dq = []
     for i in range(JOIN):
@@ -260,10 +295,9 @@
         dpb[rows, :n] = dp
         entered = (dob[rows].astype(F32) * ends[0, rows]).astype(BF16)
         dq.append((dot(dp, kx[:n]) + dot_nt(entered, state_in[...])).astype(BF16))
-    snd2[:, :HD] = dot(ut_ref[...], jnp.concatenate(dq, axis=0)).astype(BF16)
-    send_back(0, HD, 9)
-    mates(lambda m, p: remote(nsend.at[m], nrm_ref.at[:, own_cols], 7, ctx=p).start())
-    nrm_ref[:, own_cols] = nsend[k]
+    sndq[...] = dot(ut_ref[...], jnp.concatenate(dq, axis=0)).astype(BF16)
+    send_back(sndq, rcvq, 10)
+    rcvq[k, pl.ds(grp * CAP, CAP)] = sndq[pl.ds(c * CAP, CAP)]
 
     wait(back_in, rsem, 8)
     dk, dv = [], []
@@ -275,49 +309,94 @@
         dk.append((dot_tn(dpb[low:, cols], qx[low:]) + dot_nt(value, back_in[...])).astype(BF16))
         dv.append((dot_tn(pb[low:, cols], dob[low:]) + dot(key, back_in[...])).astype(BF16))
     both = jnp.concatenate([jnp.concatenate(dk, axis=0), jnp.concatenate(dv, axis=0)], axis=1)
-    snd2[:, HD:] = dot(ut_ref[...], both).astype(BF16)
-    send_back(HD, 2 * HD, 10)
-    rcv2[k, pl.ds(grp * CAP, CAP)] = snd2[pl.ds(c * CAP, CAP)]
-
-    give = onehot(iota((ROWS, SLOTS), 1) == slot_col)
-    wait(snd2.at[pl.ds(0, ARRIVE - CAP), pl.ds(0, HD)], rsem, 9)
+    snd2[...] = dot(ut_ref[...], both).astype(BF16)
+    send_back(snd2, got, 11)
+    stores.append(
+        pltpu.make_async_copy(snd2.at[pl.ds(c * CAP, CAP)], got.at[k, pl.ds(grp * CAP, CAP)], lsem.at[9])
+    )
+    stores[-1].start()
+
+    wait(att.at[pl.ds(0, SPAN - ROWS)], rsem, 7)
+    inv = column(inv_ref[:, own_cols])
     for h in range(JOIN):
-        dq_ref[:, h * HD : (h + 1) * HD] = dot(give, rcv2[h, :, :HD]).astype(BF16)
-    wait(snd2.at[pl.ds(0, ARRIVE - CAP), pl.ds(HD, 2 * HD)], rsem, 10)
+        cols = slice(h * HD, (h + 1) * HD)
+        nrm_ref[:, cols] = (attx[:, cols].astype(F32) * inv * gain_ref[:, cols]).astype(BF16)
+    stores.append(pltpu.make_async_copy(nrm_ref, nrm_out, lsem.at[10]))
+    stores[-1].start()
+
+    wait(sndq.at[pl.ds(0, ARRIVE - CAP)], rsem, 10)
     for h in range(JOIN):
-        moved = dot(give, rcv2[h, :, HD:]).astype(BF16)
-        dk_ref[:, h * HD : (h + 1) * HD] = moved[:, :HD]
-        dv_ref[:, h * HD : (h + 1) * HD] = moved[:, HD:]
-    wait(nsend.at[pl.ds(0, JOIN - 1)], rsem, 7)
-
-    wait(plr.at[pl.ds(0, CTX - 1)], ssem, 0)
+        dq_ref[:, h * HD : (h + 1) * HD] = dot(give_ref[...], rcvq[h]).astype(BF16)
+    stores.append(pltpu.make_async_copy(dq_ref, dq_out, lsem.at[11]))
+    stores[-1].start()
+    wait(snd2.at[pl.ds(0, ARRIVE - CAP)], rsem, 11)
+
+    wait(pall.at[pl.ds(0, 15)], ssem, 0)
     wait(rcv.at[pl.ds(0, ARRIVE - CAP), pl.ds(0, 2 * HD)], ssem, 1)
     wait(rcv.at[pl.ds(0, ARRIVE - CAP), pl.ds(2 * HD, HD)], ssem, 2)
     wait(gox.at[pl.ds(0, SPAN - ROWS)], ssem, 3)
     wait(state, ssem, 4)
     wait(ar1.at[pl.ds(0, JOIN - 1)], ssem, 5)
     wait(ar2.at[pl.ds(0, TP - 1)], ssem, 6)
-    wait(nsend.at[pl.ds(0, JOIN - 1)], ssem, 7)
+    wait(att.at[pl.ds(0, SPAN - ROWS)], ssem, 7)
     wait(back, ssem, 8)
-    wait(snd2.at[pl.ds(0, ARRIVE - CAP), pl.ds(0, HD)], ssem, 9)
-    wait(snd2.at[pl.ds(0, ARRIVE - CAP), pl.ds(HD, 2 * HD)], ssem, 10)
+    wait(pall.at[pl.ds(0, 48)], ssem, 9)
+    wait(sndq.at[pl.ds(0, ARRIVE - CAP)], ssem, 10)
+    wait(snd2.at[pl.ds(0, ARRIVE - CAP)], ssem, 11)
+    for store in stores:
+        store.wait()
+
+
+def finish(nrm, dq, got, give, nrm_out, dq_out, dk_out, dv_out, *scratch):
+    nrm_ref, dq_ref, got_ref, give_ref, dk_ref, dv_ref, sem = scratch
+    loads = [
+        pltpu.make_async_copy(src, dst, sem.at[i])
+        for i, (src, dst) in enumerate(((give, give_ref), (got, got_ref), (nrm, nrm_ref), (dq, dq_ref)))
+    ]
+    stores = [
+        pltpu.make_async_copy(src, dst, sem.at[4 + i])
+        for i, (src, dst) in enumerate(((dk_ref, dk_out), (dv_ref, dv_out), (nrm_ref, nrm_out), (dq_ref, dq_out)))
+    ]
+    for load in loads:
+        load.start()
+    for load in loads[:2]:
+        load.wait()
+    for i, ref in enumerate((dk_ref, dv_ref)):
+        for h in range(JOIN):
+            moved = dot(give_ref[...], got_ref[h, :, i * HD : (i + 1) * HD])
+            ref[:, h * HD : (h + 1) * HD] = moved.astype(BF16)
+        stores[i].start()
+    for load, store in zip(loads[2:], stores[2:]):
+        load.wait()
+        store.start()
+    for store in stores:
+        store.wait()
 
 
 def body(query_rows, key_rows, value_rows, position, lengths, decay_rates, norm_gain, grad_output):
-    vmem, smem = pl.BlockSpec(memory_space=pltpu.VMEM), pl.BlockSpec(memory_space=pltpu.SMEM)
+    hbm = pl.BlockSpec(memory_space=pltpu.HBM)
     shape = jax.ShapeDtypeStruct(query_rows.shape, BF16)
-    return pl.pallas_call(
+    held = pltpu.VMEM(query_rows.shape, BF16)
+    kept = pl.pallas_call(
         kernel,
-        out_shape=(shape,) * 4,
-        in_specs=[vmem, smem, smem] + [vmem] * 5,
-        out_specs=(vmem,) * 4,
+        out_shape=(
+            shape, shape,
+            jax.ShapeDtypeStruct((JOIN, SLOTS, 2 * HD), BF16), jax.ShapeDtypeStruct((ROWS, SLOTS), BF16),
+        ),
+        in_specs=[hbm] * 8,
+        out_specs=(hbm,) * 4,
         scratch_shapes=[
+            pltpu.VMEM((1, ROWS), I32),
+            pltpu.SMEM(lengths.shape, I32),
+            pltpu.SMEM(decay_rates.shape, F32),
+            pltpu.VMEM((1, JOIN * HD), F32),
+            held, held, held, held,
+            pltpu.SemaphoreType.DMA((12,)),
             pltpu.VMEM((GROUPS, JOIN, CAP, WIDE), BF16),
             pltpu.VMEM((ARRIVE, WIDE), BF16),
-            pltpu.VMEM((ARRIVE, WIDE), BF16),
-            pltpu.VMEM((JOIN, SLOTS, WIDE), BF16),
-            pltpu.VMEM((GROUPS, ROWS), F32),
-            pltpu.VMEM((CTX, ROWS), F32),
+            pltpu.VMEM((ARRIVE, HD), BF16),
+            pltpu.VMEM((ARRIVE, 2 * HD), BF16),
+            pltpu.VMEM((CTX, ROWS), I32),
             pltpu.VMEM((SPAN, ARRIVE), BF16),
             pltpu.VMEM((ARRIVE, SPAN), BF16),
             pltpu.VMEM((SPAN, SPAN), F32),
@@ -327,10 +406,13 @@
             pltpu.VMEM((SPAN, HD), BF16),
             pltpu.VMEM((SPAN, HD), BF16),
             pltpu.VMEM((SPAN, HD), BF16),
+            held,
             pltpu.VMEM((SPAN, HD), BF16),
             pltpu.VMEM((SPAN, SPAN), BF16),
             pltpu.VMEM((SPAN, SPAN), BF16),
-            pltpu.VMEM((JOIN, ROWS, HD), BF16),
+            held, held,
+            pltpu.VMEM((ROWS, SLOTS), BF16),
+            pltpu.VMEM((JOIN, SLOTS, HD), BF16),
             pltpu.VMEM((HD, HD), BF16),
             pltpu.VMEM((HD, HD), BF16),
             pltpu.VMEM((HD, HD), BF16),
@@ -339,17 +421,30 @@
             pltpu.VMEM((JOIN, 1, 2 * SPAN), F32),
             pltpu.VMEM((1, 2 * SPAN), F32),
             pltpu.VMEM((TP, 1, 2 * SPAN), F32),
-            pltpu.SemaphoreType.DMA((11,)),
-            pltpu.SemaphoreType.DMA((11,)),
+            pltpu.VMEM((1, SPAN), F32),
+            pltpu.SemaphoreType.DMA((12,)),
+            pltpu.SemaphoreType.DMA((12,)),
         ],
         compiler_params=pltpu.CompilerParams(
-            collective_id=0, has_side_effects=True, vmem_limit_bytes=40 << 20
+            collective_id=0, has_side_effects=True, vmem_limit_bytes=60 << 20
         ),
         name="lightning",
     )(
         position.reshape(1, ROWS), lengths, decay_rates, norm_gain.reshape(1, -1),
         query_rows, key_rows, value_rows, grad_output,
     )
+    return pl.pallas_call(
+        finish,
+        out_shape=(shape,) * 4,
+        in_specs=[hbm] * 4,
+        out_specs=(hbm,) * 4,
+        scratch_shapes=[
+            held, held, pltpu.VMEM((JOIN, SLOTS, 2 * HD), BF16), pltpu.VMEM((ROWS, SLOTS), BF16),
+            held, held, pltpu.SemaphoreType.DMA((8,)),
+        ],
+        compiler_params=pltpu.CompilerParams(vmem_limit_bytes=60 << 20),
+        name="finish",
+    )(*kept)
 
 
 def solution(mesh):

time: 122 us -> 111 us (0.910)
  local copies, waits for them, and re-layouts: 6.91 us -> 0 us
  Pallas kernels: 115 us -> 110 us
    unnamed x20 -> x0, local copies, waits for them, and re-layouts: 6.91 us -> none
    pallas_call x1 -> x2, Pallas kernels: 115 us -> 110 us  [the longest x1 108 us: body(): pl.pallas_call(kernel, out_shape=(shape, shape, jax.ShapeDtypeStruct((JOI...]
where the time goes in v2:
time: 111 us
  Pallas kernels  110 us (99%)
    pallas_call x1, Pallas kernels, body(): pl.pallas_call(kernel, out_shape=(shape, shape, jax.ShapeDtypeStruct((JOI...  108 us

profile of v2, /device:TPU:1, one launch (start us, length us, event | category | flops | bytes accessed | tf_op | source)
XLA Modules:
  0.0 110.9 jit_solution(16435879662870611951)
XLA Ops:
  0.6 108.1 %lightning.1 = (bf16[128,512]{1,0:T(8,128)(2,1)}, bf16[128,512]{1,0:T(8,128)(2,1)}, bf16[4,256,256]{2,1,0:T(8,128)(2,1)}, bf16[128,256]{1,0:T(8,128)(2,1)}) custom-call(s32[1,128]{1,0:T(1,128)} %bitcast.3, s32[32]{0:T(128)} %len_hbm.1, f32[4]{0:T(128)} %rate_hbm.1, f32[1,512]{1,0:T(1,128)} %bitcast.2, bf16[128,512]{1,0:T(8,128)(2,1)} %q_hbm.1, ...), custom_call_target="tpu_custom_call" | custom-call | tf_op jit(solution)/shard_map/lightning/pallas_call | solution.py:380
  108.7 2.2 %finish.1 = (bf16[128,512]{1,0:T(8,128)(2,1)}, bf16[128,512]{1,0:T(8,128)(2,1)}, bf16[128,512]{1,0:T(8,128)(2,1)}, bf16[128,512]{1,0:T(8,128)(2,1)}) custom-call(bf16[128,512]{1,0:T(8,128)(2,1)} %get-tuple-element.8.nrm, bf16[128,512]{1,0:T(8,128)(2,1)} %get-tuple-element.9.dq, bf16[4,256,256]{2,1,0:T(8,128)(2,1)} %get-tuple-element.10.got, ...), custom_call_target="tpu_custom_call" | custom-call | tf_op jit(solution)/shard_map/finish/pallas_call | solution.py:436

commit v3 on v2

--- a/solution.py
+++ b/solution.py
@@ -50,7 +50,7 @@
     nrm_out, dq_out, got, give_out,
     pos_ref, len_ref, rate_ref, gain_ref, q_ref, k_ref, v_ref, go_ref, lsem,
     snd, rcv, sndq, snd2, pall, u_ref, ut_ref, w_ref, ends, qx, kx, vx, gox, att, attx, dob, pb, dpb,
-    nrm_ref, dq_ref, give_ref, rcvq, state, state_in, back, back_in, part, ar1, sub, ar2, inv_ref, ssem, rsem,
+    nrm_ref, dq_ref, give_ref, rcvq, state, state_in, back, back_in, part, parts, inv_ref, ssem, rsem, known,
 ):
     c, t = lax.axis_index("ctx"), lax.axis_index("tp")
     grp, k = c // JOIN, lax.rem(c, JOIN)
@@ -67,15 +67,34 @@
     ]
     for load in loads:
         load.start()
+    own_y, own_z = c // 16, lax.rem(c, 16)
+
+    def step_to(dy, dz):
+        return lax.rem(own_y + dy, 4) * 16 + lax.rem(own_z + dz, 16)
+
+    def peer(f):
+        turn = f // 4
+        h = (turn + 1) // 2
+        return step_to(lax.rem(f, 4), jnp.where(lax.rem(turn, 2) == 1, h, 16 - h))
+
     barrier = pltpu.get_barrier_semaphore()
-
-    @pl.loop(1, CTX)
-    def _(d):
-        pl.semaphore_signal(barrier, inc=1, device_id={"ctx": lax.rem(c + d, CTX)}, device_id_type=MESH)
+    near = 12
+
+    @pl.loop(1, near)
+    def _(f):
+        pl.semaphore_signal(barrier, inc=1, device_id={"ctx": peer(f)}, device_id_type=MESH)
 
     @pl.loop(1, TP)
     def _(d):
         pl.semaphore_signal(barrier, inc=1, device_id={"tp": lax.rem(t + d, TP)}, device_id_type=MESH)
+
+    def tell(reach, i):
+        for j, dz in enumerate((16 - reach, reach)):
+            pl.semaphore_signal(known.at[2 * i + j], inc=1, device_id={"ctx": step_to(0, dz)}, device_id_type=MESH)
+
+    def learn(i):
+        for j in range(2):
+            pl.semaphore_wait(known.at[2 * i + j], 1)
 
     def remote(src, dst, index, **where):
         return pltpu.make_async_remote_copy(
@@ -85,13 +104,6 @@
 
     def wait(ref, sems, index):
         pltpu.make_async_copy(ref, ref, sems.at[index]).wait()
-
-    def peer(d):
-        f = CTX - d
-        turn, dy = f // 4, lax.rem(f, 4)
-        h = (turn + 1) // 2
-        dz = jnp.where(lax.rem(turn, 2) == 1, h, 16 - h)
-        return lax.rem(c // 16 + dy, 4) * 16 + lax.rem(lax.rem(c, 16) + dz, 16)
 
     loads[0].wait()
     pos = pos_ref[...]
@@ -113,29 +125,48 @@
                 GROUPS, CAP, HD
             )
 
-    for i, ref in enumerate((k_ref, v_ref, q_ref)):
+    def send_rows(f, lo, n, index):
+        p = peer(f)
+        remote(
+            snd.at[p // JOIN, lax.rem(p, JOIN), :, pl.ds(lo, n)],
+            rcv.at[pl.ds(c * CAP, CAP), pl.ds(lo, n)],
+            index, ctx=p,
+        ).start()
+
+    def send_stage(first, last):
+        @pl.loop((first + 3) // 4, last // 4)
+        def _(turn):
+            remote(pos_ref, pall.at[pl.ds(c, 1)], 0, ctx=peer(4 * turn)).start()
+
+        @pl.loop(first, last)
+        def _(i):
+            send_rows(last - 1 + first - i, 0, 2 * HD, 1)
+
+    pl.semaphore_wait(barrier, near - 1 + TP - 1)
+    tell(1, 0)
+    for i, ref in enumerate((k_ref, v_ref)):
         loads[i + 1].wait()
         spread(ref, i)
-    pl.semaphore_wait(barrier, CTX - 1 + TP - 1)
-
-    own_y, own_z = c // 16, lax.rem(c, 16)
-
-    @pl.loop(1, 16)
+    send_stage(1, near)
+    learn(0)
+    tell(2, 1)
+    send_stage(near, 20)
+    learn(1)
+    tell(4, 2)
+
+    @pl.loop(1, TP)
     def _(d):
-        remote(pos_ref, pall.at[pl.ds(c, 1)], 0, ctx=own_y * 16 + lax.rem(own_z + d, 16)).start()
-
-    def send_rows(lo, n, index):
-        @pl.loop(1, CTX)
-        def _(d):
-            p = peer(d)
-            remote(
-                snd.at[p // JOIN, lax.rem(p, JOIN), :, pl.ds(lo, n)],
-                rcv.at[pl.ds(c * CAP, CAP), pl.ds(lo, n)],
-                index, ctx=p,
-            ).start()
-
-    send_rows(0, 2 * HD, 1)
-    send_rows(2 * HD, HD, 2)
+        pl.semaphore_signal(known.at[6], inc=1, device_id={"tp": lax.rem(t + d, TP)}, device_id_type=MESH)
+
+    send_stage(20, 36)
+    loads[3].wait()
+    spread(q_ref, 2)
+    learn(2)
+    send_stage(36, CTX)
+
+    @pl.loop(1, CTX)
+    def _(i):
+        send_rows(CTX - i, 2 * HD, HD, 2)
 
     def mates(fn):
         for d in range(1, JOIN):
@@ -214,13 +245,13 @@
     vx[...] = kv[:, HD:]
     state[...] = dot_tn((kx[...].astype(F32) * ends[2]).astype(BF16), vx[...]).astype(BF16)
     remote(state, state_in, 4, ctx=lax.rem(c + JOIN, CTX)).start()
-
-    wait(rcv.at[pl.ds(0, ARRIVE - CAP), pl.ds(2 * HD, HD)], rsem, 2)
     mates(
         lambda m, p: remote(
             go_ref.at[:, pl.ds(pl.multiple_of(m * HD, HD), HD)], gox.at[pl.ds(k * ROWS, ROWS)], 3, ctx=p
         ).start()
     )
+
+    wait(rcv.at[pl.ds(0, ARRIVE - CAP), pl.ds(2 * HD, HD)], rsem, 2)
     qx[...] = dot(u_ref[...], rcv[:, 2 * HD :]).astype(BF16)
     for i in range(JOIN):
         rows, n = slice(i * ROWS, (i + 1) * ROWS), (i + 1) * ROWS
@@ -240,40 +271,38 @@
         a = (dot(pb[rows, :n], vx[:n]) + dot(entered, state_in[...])).astype(BF16)
         att[rows] = a
         a = a.astype(F32)
-        part[:, i * ROWS : (i + 1) * ROWS] = row_sums(a * a)
+        part[i : i + 1] = row_sums(a * a)
     wait(gox.at[pl.ds(0, SPAN - ROWS)], rsem, 3)
     for i in range(JOIN):
         rows = slice(i * ROWS, (i + 1) * ROWS)
         g = gox[rows].astype(F32) * gain
-        part[:, SPAN + i * ROWS : SPAN + (i + 1) * ROWS] = row_sums(g * att[rows].astype(F32))
-
-    for d in range(1, TP):
-        remote(part, ar2.at[t], 6, tp=lax.rem(t + d, TP)).start()
+        part[JOIN + i : JOIN + i + 1] = row_sums(g * att[rows].astype(F32))
+
+    pl.semaphore_wait(known.at[6], TP - 1)
+
+    @pl.loop(1, JOIN * TP)
+    def _(i):
+        m = lax.rem(k + i // TP, JOIN)
+        remote(part, parts.at[k * TP + t], 5, ctx=grp * JOIN + m, tp=lax.rem(t + i, TP)).start()
+
     mates(
         lambda m, p: remote(
             att.at[pl.ds(pl.multiple_of(m * ROWS, ROWS), ROWS)], attx.at[:, own_cols], 7, ctx=p
         ).start()
     )
     attx[:, own_cols] = att[pl.ds(pl.multiple_of(k * ROWS, ROWS), ROWS)]
-    ar2[t] = part[...]
-    wait(ar2.at[pl.ds(0, TP - 1)], rsem, 6)
-    total = ar2[0]
-    for d in range(1, TP):
-        total += ar2[d]
-    sub[...] = total
-    mates(lambda m, p: remote(sub, ar1.at[k], 5, ctx=p).start())
-    ar1[k] = total
-    wait(ar1.at[pl.ds(0, JOIN - 1)], rsem, 5)
-    total = ar1[0] + ar1[1] + ar1[2] + ar1[3]
+    parts[k * TP + t] = part[...]
+    wait(parts.at[pl.ds(0, JOIN * TP - 1)], rsem, 5)
+    total = jnp.sum(parts[...], axis=0)
     width = float(HD * JOIN * TP)
-    inverse = lax.rsqrt(total[:, :SPAN] / width + EPSILON)
-    coef = inverse * inverse * inverse * total[:, SPAN:] / width
+    inverse = lax.rsqrt(total[:JOIN] / width + EPSILON)
+    coef = inverse * inverse * inverse * total[JOIN:] / width
     inv_ref[...] = inverse
 
     carried = jnp.zeros((HD, HD), F32)
     for i in range(JOIN):
         rows = slice(i * ROWS, (i + 1) * ROWS)
-        inv, cf = column(inverse[:, rows]), column(coef[:, rows])
+        inv, cf = column(inverse[i : i + 1]), column(coef[i : i + 1])
         a = att[rows].astype(F32)
         g = gox[rows].astype(F32) * gain
         d_o = (inv * g - a * cf).astype(BF16)
@@ -285,7 +314,7 @@
     def send_back(src, dst, index):
         @pl.loop(1, CTX)
         def _(d):
-            p = peer(d)
+            p = peer(CTX - d)
             remote(src.at[pl.ds(p * CAP, CAP)], dst.at[k, pl.ds(grp * CAP, CAP)], index, ctx=p).start()
 
     dq = []
@@ -317,7 +346,7 @@
     stores[-1].start()
 
     wait(att.at[pl.ds(0, SPAN - ROWS)], rsem, 7)
-    inv = column(inv_ref[:, own_cols])
+    inv = column(inv_ref[pl.ds(k, 1)])
     for h in range(JOIN):
         cols = slice(h * HD, (h + 1) * HD)
         nrm_ref[:, cols] = (attx[:, cols].astype(F32) * inv * gain_ref[:, cols]).astype(BF16)
@@ -336,8 +365,7 @@
     wait(rcv.at[pl.ds(0, ARRIVE - CAP), pl.ds(2 * HD, HD)], ssem, 2)
     wait(gox.at[pl.ds(0, SPAN - ROWS)], ssem, 3)
     wait(state, ssem, 4)
-    wait(ar1.at[pl.ds(0, JOIN - 1)], ssem, 5)
-    wait(ar2.at[pl.ds(0, TP - 1)], ssem, 6)
+    wait(parts.at[pl.ds(0, JOIN * TP - 1)], ssem, 5)
     wait(att.at[pl.ds(0, SPAN - ROWS)], ssem, 7)
     wait(back, ssem, 8)
     wait(pall.at[pl.ds(0, 48)], ssem, 9)
@@ -417,13 +445,12 @@
             pltpu.VMEM((HD, HD), BF16),
             pltpu.VMEM((HD, HD), BF16),
             pltpu.VMEM((HD, HD), BF16),
-            pltpu.VMEM((1, 2 * SPAN), F32),
-            pltpu.VMEM((JOIN, 1, 2 * SPAN), F32),
-            pltpu.VMEM((1, 2 * SPAN), F32),
-            pltpu.VMEM((TP, 1, 2 * SPAN), F32),
-            pltpu.VMEM((1, SPAN), F32),
+            pltpu.VMEM((2 * JOIN, ROWS), F32),
+            pltpu.VMEM((JOIN * TP, 2 * JOIN, ROWS), F32),
+            pltpu.VMEM((JOIN, ROWS), F32),
             pltpu.SemaphoreType.DMA((12,)),
             pltpu.SemaphoreType.DMA((12,)),
+            pltpu.SemaphoreType.REGULAR((7,)),
         ],
         compiler_params=pltpu.CompilerParams(
             collective_id=0, has_side_effects=True, vmem_limit_bytes=60 << 20

time: 111 us -> 107 us (0.964)
  Pallas kernels: 110 us -> 106 us
    pallas_call x1, Pallas kernels: 108 us -> 104 us  [body(): pl.pallas_call(kernel, out_shape=(shape, shape, jax.ShapeDtypeStruct((JOI...]
where the time goes in v3:
time: 107 us
  Pallas kernels  106 us (99%)
    pallas_call x1, Pallas kernels, body(): pl.pallas_call(kernel, out_shape=(shape, shape, jax.ShapeDtypeStruct((JOI...  104 us
    pallas_call x1, Pallas kernels, body(): pl.pallas_call(finish, out_shape=(shape,) * 4, in_specs=[hbm] * 4, out_sp...  2.18 us

profile of v3, /device:TPU:1, one launch (start us, length us, event | category | flops | bytes accessed | tf_op | source)
XLA Modules:
  0.0 106.8 jit_solution(9809889296988819625)
XLA Ops:
  0.6 104.0 %lightning.1 = (bf16[128,512]{1,0:T(8,128)(2,1)}, bf16[128,512]{1,0:T(8,128)(2,1)}, bf16[4,256,256]{2,1,0:T(8,128)(2,1)}, bf16[128,256]{1,0:T(8,128)(2,1)}) custom-call(s32[1,128]{1,0:T(1,128)} %bitcast.3, s32[32]{0:T(128)} %len_hbm.1, f32[4]{0:T(128)} %rate_hbm.1, f32[1,512]{1,0:T(1,128)} %bitcast.2, bf16[128,512]{1,0:T(8,128)(2,1)} %q_hbm.1, ...), custom_call_target="tpu_custom_call" | custom-call | tf_op jit(solution)/shard_map/lightning/pallas_call | solution.py:408
  104.7 2.2 %finish.1 = (bf16[128,512]{1,0:T(8,128)(2,1)}, bf16[128,512]{1,0:T(8,128)(2,1)}, bf16[128,512]{1,0:T(8,128)(2,1)}, bf16[128,512]{1,0:T(8,128)(2,1)}) custom-call(bf16[128,512]{1,0:T(8,128)(2,1)} %get-tuple-element.8.nrm, bf16[128,512]{1,0:T(8,128)(2,1)} %get-tuple-element.9.dq, bf16[4,256,256]{2,1,0:T(8,128)(2,1)} %get-tuple-element.10.got, ...), custom_call_target="tpu_custom_call" | custom-call | tf_op jit(solution)/shard_map/finish/pallas_call | solution.py:463

commit v4 on v3

--- a/solution.py
+++ b/solution.py
@@ -244,7 +244,8 @@
     kx[...] = kv[:, :HD]
     vx[...] = kv[:, HD:]
     state[...] = dot_tn((kx[...].astype(F32) * ends[2]).astype(BF16), vx[...]).astype(BF16)
-    remote(state, state_in, 4, ctx=lax.rem(c + JOIN, CTX)).start()
+    for i in range(0, HD, 16):
+        remote(state.at[pl.ds(i, 16)], state_in.at[pl.ds(i, 16)], 4, ctx=lax.rem(c + JOIN, CTX)).start()
     mates(
         lambda m, p: remote(
             go_ref.at[:, pl.ds(pl.multiple_of(m * HD, HD), HD)], gox.at[pl.ds(k * ROWS, ROWS)], 3, ctx=p
@@ -309,13 +310,22 @@
         dob[rows] = d_o
         carried += dot_tn((qx[rows].astype(F32) * ends[3, rows]).astype(BF16), d_o)
     back[...] = carried.astype(BF16)
-    remote(back, back_in, 8, ctx=lax.rem(c + CTX - JOIN, CTX)).start()
-
-    def send_back(src, dst, index):
+    for i in range(0, HD, 16):
+        remote(back.at[pl.ds(i, 16)], back_in.at[pl.ds(i, 16)], 8, ctx=lax.rem(c + CTX - JOIN, CTX)).start()
+
+    def send_back(src, dst, index, early):
+        def send(p):
+            remote(src.at[pl.ds(p * CAP, CAP)], dst.at[k, pl.ds(grp * CAP, CAP)], index, ctx=p).start()
+
+        @pl.loop(0, 4 * early)
+        def _(i):
+            p = lax.rem(own_y + i, 4) * 16 + i // 4
+            pl.when(p != c)(lambda: send(p))
+
         @pl.loop(1, CTX)
         def _(d):
             p = peer(CTX - d)
-            remote(src.at[pl.ds(p * CAP, CAP)], dst.at[k, pl.ds(grp * CAP, CAP)], index, ctx=p).start()
+            pl.when(lax.rem(p, 16) >= early)(lambda: send(p))
 
     dq = []
     for i in range(JOIN):
@@ -325,7 +335,7 @@
         entered = (dob[rows].astype(F32) * ends[0, rows]).astype(BF16)
         dq.append((dot(dp, kx[:n]) + dot_nt(entered, state_in[...])).astype(BF16))
     sndq[...] = dot(ut_ref[...], jnp.concatenate(dq, axis=0)).astype(BF16)
-    send_back(sndq, rcvq, 10)
+    send_back(sndq, rcvq, 10, 6)
     rcvq[k, pl.ds(grp * CAP, CAP)] = sndq[pl.ds(c * CAP, CAP)]
 
     wait(back_in, rsem, 8)
@@ -339,7 +349,7 @@
         dv.append((dot_tn(pb[low:, cols], dob[low:]) + dot(key, back_in[...])).astype(BF16))
     both = jnp.concatenate([jnp.concatenate(dk, axis=0), jnp.concatenate(dv, axis=0)], axis=1)
     snd2[...] = dot(ut_ref[...], both).astype(BF16)
-    send_back(snd2, got, 11)
+    send_back(snd2, got, 11, 6)
     stores.append(
         pltpu.make_async_copy(snd2.at[pl.ds(c * CAP, CAP)], got.at[k, pl.ds(grp * CAP, CAP)], lsem.at[9])
     )

time: 107 us -> 103 us (0.963)
  the two profiles are of different devices: /device:TPU:1 before, /device:TPU:128 now
where the time goes in v4:
time: 103 us
  Pallas kernels  102 us (99%)
    pallas_call x1, Pallas kernels, body(): pl.pallas_call(kernel, out_shape=(shape, shape, jax.ShapeDtypeStruct((JOI...  99.9 us
    pallas_call x1, Pallas kernels, body(): pl.pallas_call(finish, out_shape=(shape,) * 4, in_specs=[hbm] * 4, out_sp...  2.18 us

profile of v4, /device:TPU:128, one launch (start us, length us, event | category | flops | bytes accessed | tf_op | source)
XLA Modules:
  0.0 102.7 jit_solution(5901033213025103463)
XLA Ops:
  0.6 99.9 %lightning.1 = (bf16[128,512]{1,0:T(8,128)(2,1)}, bf16[128,512]{1,0:T(8,128)(2,1)}, bf16[4,256,256]{2,1,0:T(8,128)(2,1)}, bf16[128,256]{1,0:T(8,128)(2,1)}) custom-call(s32[1,128]{1,0:T(1,128)} %bitcast.3, s32[32]{0:T(128)} %len_hbm.1, f32[4]{0:T(128)} %rate_hbm.1, f32[1,512]{1,0:T(1,128)} %bitcast.2, bf16[128,512]{1,0:T(8,128)(2,1)} %q_hbm.1, ...), custom_call_target="tpu_custom_call" | custom-call | tf_op jit(solution)/shard_map/lightning/pallas_call | solution.py:418
  100.5 2.2 %finish.1 = (bf16[128,512]{1,0:T(8,128)(2,1)}, bf16[128,512]{1,0:T(8,128)(2,1)}, bf16[128,512]{1,0:T(8,128)(2,1)}, bf16[128,512]{1,0:T(8,128)(2,1)}) custom-call(bf16[128,512]{1,0:T(8,128)(2,1)} %get-tuple-element.8.nrm, bf16[128,512]{1,0:T(8,128)(2,1)} %get-tuple-element.9.dq, bf16[4,256,256]{2,1,0:T(8,128)(2,1)} %get-tuple-element.10.got, ...), custom_call_target="tpu_custom_call" | custom-call | tf_op jit(solution)/shard_map/finish/pallas_call | solution.py:473

commit v5 on v4

--- a/solution.py
+++ b/solution.py
@@ -387,26 +387,30 @@
 
 def finish(nrm, dq, got, give, nrm_out, dq_out, dk_out, dv_out, *scratch):
     nrm_ref, dq_ref, got_ref, give_ref, dk_ref, dv_ref, sem = scratch
+    halves = [(got.at[:, :, pl.ds(i * HD, HD)], got_ref.at[i]) for i in range(2)]
     loads = [
         pltpu.make_async_copy(src, dst, sem.at[i])
-        for i, (src, dst) in enumerate(((give, give_ref), (got, got_ref), (nrm, nrm_ref), (dq, dq_ref)))
+        for i, (src, dst) in enumerate([(give, give_ref)] + halves + [(nrm, nrm_ref), (dq, dq_ref)])
     ]
     stores = [
-        pltpu.make_async_copy(src, dst, sem.at[4 + i])
+        pltpu.make_async_copy(src, dst, sem.at[5 + i])
         for i, (src, dst) in enumerate(((dk_ref, dk_out), (dv_ref, dv_out), (nrm_ref, nrm_out), (dq_ref, dq_out)))
     ]
     for load in loads:
         load.start()
-    for load in loads[:2]:
-        load.wait()
-    for i, ref in enumerate((dk_ref, dv_ref)):
+    loads[0].wait()
+
+    def moved(i, ref):
+        loads[1 + i].wait()
         for h in range(JOIN):
-            moved = dot(give_ref[...], got_ref[h, :, i * HD : (i + 1) * HD])
-            ref[:, h * HD : (h + 1) * HD] = moved.astype(BF16)
+            ref[:, h * HD : (h + 1) * HD] = dot(give_ref[...], got_ref[i, h]).astype(BF16)
         stores[i].start()
-    for load, store in zip(loads[2:], stores[2:]):
+
+    moved(0, dk_ref)
+    for load, store in zip(loads[3:], stores[2:]):
         load.wait()
         store.start()
+    moved(1, dv_ref)
     for store in stores:
         store.wait()
 
@@ -476,8 +480,8 @@
         in_specs=[hbm] * 4,
         out_specs=(hbm,) * 4,
         scratch_shapes=[
-            held, held, pltpu.VMEM((JOIN, SLOTS, 2 * HD), BF16), pltpu.VMEM((ROWS, SLOTS), BF16),
-            held, held, pltpu.SemaphoreType.DMA((8,)),
+            held, held, pltpu.VMEM((2, JOIN, SLOTS, HD), BF16), pltpu.VMEM((ROWS, SLOTS), BF16),
+            held, held, pltpu.SemaphoreType.DMA((9,)),
         ],
         compiler_params=pltpu.CompilerParams(vmem_limit_bytes=60 << 20),
         name="finish",

time: 103 us -> 103 us (level)
  no operation moved by 1% of the time
where the time goes in v5:
time: 103 us
  Pallas kernels  102 us (99%)
    pallas_call x1, Pallas kernels, body(): pl.pallas_call(kernel, out_shape=(shape, shape, jax.ShapeDtypeStruct((JOI...  99.9 us
    pallas_call x1, Pallas kernels, body(): pl.pallas_call(finish, out_shape=(shape,) * 4, in_specs=[hbm] * 4, out_sp...  2.17 us

profile of v5, /device:TPU:128, one launch (start us, length us, event | category | flops | bytes accessed | tf_op | source)
XLA Modules:
  0.0 102.7 jit_solution(1449397667663807881)
XLA Ops:
  0.6 99.9 %lightning.1 = (bf16[128,512]{1,0:T(8,128)(2,1)}, bf16[128,512]{1,0:T(8,128)(2,1)}, bf16[4,256,256]{2,1,0:T(8,128)(2,1)}, bf16[128,256]{1,0:T(8,128)(2,1)}) custom-call(s32[1,128]{1,0:T(1,128)} %bitcast.3, s32[32]{0:T(128)} %len_hbm.1, f32[4]{0:T(128)} %rate_hbm.1, f32[1,512]{1,0:T(1,128)} %bitcast.2, bf16[128,512]{1,0:T(8,128)(2,1)} %q_hbm.1, ...), custom_call_target="tpu_custom_call" | custom-call | tf_op jit(solution)/shard_map/lightning/pallas_call | solution.py:422
  100.5 2.2 %finish.1 = (bf16[128,512]{1,0:T(8,128)(2,1)}, bf16[128,512]{1,0:T(8,128)(2,1)}, bf16[128,512]{1,0:T(8,128)(2,1)}, bf16[128,512]{1,0:T(8,128)(2,1)}) custom-call(bf16[128,512]{1,0:T(8,128)(2,1)} %get-tuple-element.8.nrm, bf16[128,512]{1,0:T(8,128)(2,1)} %get-tuple-element.9.dq, bf16[4,256,256]{2,1,0:T(8,128)(2,1)} %get-tuple-element.10.got, ...), custom_call_target="tpu_custom_call" | custom-call | tf_op jit(solution)/shard_map/finish/pallas_call | solution.py:477
